TPU v7x, 256 devices: a whole 4x4x8 slice. The times are simulated.
256 devices in a mesh: row: 32 (over x, z_hi, core), feat: 8 (over y, z_lo).
Axes of the slice: x: 4, y: 4, z: 8 (z_hi: 4, z_lo: 2; z = z_hi * 2 + z_lo), core: 2. Of those that a mesh axis runs over, the one named last changes fastest.
Arguments:
- features: bfloat16 [8192, 7168], P('row', 'feat'), may hold values from -6 to 6
- weights: float32 [7168], P('feat'), may hold values from -0.0625 to 0.0625
- labels: int32 [8192], P('row'), may hold values 0 or 1
- sign_bits: int32 [8192], P('row'), may hold values 0 or 1
- sample_rows: int32 [7680], P('row'), may hold values from 0 to 255, as said below
Outputs:
- gram: float32 [7168, 7168], P('row', 'feat')
- gradient: float32 [7168], P('feat')
Inputs may be any that keep to these rules, and one draw needn't show every extreme that they name: `sample_rows`: each block of 240 entries is strictly rising, starts at 0 and ends at 255.
All inputs are finite; a program needn't handle non-finite values. No bound on the sum of `labels` or of `sign_bits` on one device may be relied on, other than what follows from the above.
Results may differ from a plain program's by a relative error of at most 0.0028.
Values may be sent and summed in bfloat16 or wider, within the bound.
A program may use at most 128 MiB of HBM per device.

v0:
```python
import jax
import jax.numpy as jnp
from jax import lax
from jax.sharding import PartitionSpec as P


def swapped(value, axis, apart):
    mask = 2**apart
    pairs = [(source, source ^ mask) for source in range(lax.axis_size(axis))]
    return lax.ppermute(value, axis, pairs)


def sign_table(picked, size):
    levels = size.bit_length() - 1
    columns = jnp.arange(size, dtype=jnp.int32)
    parity = jnp.zeros((picked.shape[0], size), jnp.int32)
    for level in range(levels):
        left_bit = picked[:, None] // (1 << level) % 2
        right_bit = columns[None, :] // (1 << level) % 2
        parity = parity + left_bit * right_bit
    return (1 - 2 * (parity % 2)).astype(jnp.float32)


def shards(features, weights, labels, sign_bits, sample_rows):
    highest = lax.Precision.HIGHEST
    rows_dev = features.shape[0]
    blocks = lax.axis_size("row")
    total_rows = rows_dev * blocks
    partial_logits = jnp.dot(
        features, weights, precision=highest, preferred_element_type=jnp.float32
    )
    logits = lax.psum(partial_logits, "feat")
    probability = jax.nn.sigmoid(logits)
    residual = probability - labels.astype(jnp.float32)
    grad_term = jnp.dot(residual, features, precision=highest, preferred_element_type=jnp.float32)
    gradient = lax.psum(grad_term, "row") / jnp.sqrt(jnp.float32(total_rows))
    scaling = (2 * sign_bits - 1).astype(jnp.float32) * jnp.sqrt(probability * (1.0 - probability))
    mixed_rows = scaling[:, None] * features.astype(jnp.float32)
    position = lax.axis_index("row")
    for level in range(blocks.bit_length() - 1):
        partner = swapped(mixed_rows, "row", level)
        lower = position // (1 << level) % 2 == 0
        mixed_rows = jnp.where(lower, mixed_rows + partner, partner - mixed_rows)
    table = sign_table(sample_rows, rows_dev)
    sketch = (
        jnp.dot(table, mixed_rows, precision=highest) / jnp.sqrt(jnp.float32(total_rows))
    ).astype(jnp.bfloat16)
    whole_sketch = lax.all_gather(sketch, "feat", axis=1, tiled=True)
    summed = lax.psum_scatter(
        lax.dot_general(
            whole_sketch, sketch, (((0,), (0,)), ((), ())), preferred_element_type=jnp.float32
        ),
        "row",
        scatter_dimension=0,
        tiled=True,
    )
    gram = summed / jnp.sqrt(jnp.float32(sample_rows.shape[0] * blocks))
    return (gram, gradient)


def solution(mesh):
    placed = (P("row", "feat"), P("feat"), P("row"), P("row"), P("row"))
    return jax.shard_map(
        shards, mesh=mesh, in_specs=placed, out_specs=(P("row", "feat"), P("feat")), check_vma=False
    )
```

profile of v0, /device:TPU:1, one launch (start us, length us, event | category | flops | bytes accessed | tf_op | source)
XLA Modules:
  0.0 485.8 jit_solution(11379945796981101159)
XLA Ops:
  7.2 0.0 all-gather.2.cloned.1.call-start
  7.2 0.7 reshape.570
  7.9 1.5 fusion.53
  9.4 17.5 %psum.14 = f32[256]{0:T(256)S(1)} all-reduce(f32[256]{0:T(256)S(1)} %bitcast.9), channel_id=1, replica_groups=mesh['row'=32,'feat'=8] {'feat'}, use_global_device_ids=true, to_apply=%region_0.0 | all-reduce | flops 256 | bytes 2048 | tf_op jit(solution)/shard_map/psum | solution.py:32
  26.9 0.7 convert_subtract_fusion
  27.6 1.2 convert_multiply_fusion
  28.7 4.5 collective-permute-start
  33.3 2.1 collective-permute-done
  35.4 1.2 subtract_select_fusion.3
  36.6 3.1 collective-permute-start.1
  39.7 38.7 %collective-permute-done.1 = f32[256,896]{1,0:T(8,128)S(1)} collective-permute-done((f32[256,896]{1,0:T(8,128)S(1)}, f32[256,896]{1,0:T(8,128)S(1)}, u32[]{:S(2)}, u32[]{:S(2)}) %collective-permute-start.1) | collective-permute-done | bytes 917536 | tf_op jit(solution)/shard_map/ppermute | solution.py:10
  78.3 0.1 subtract_select_fusion.2
  78.4 5.6 %collective-permute-start.2 = (f32[256,896]{1,0:T(8,128)S(1)}, f32[256,896]{1,0:T(8,128)S(1)}, u32[]{:S(2)}, u32[]{:S(2)}) collective-permute-start(f32[256,896]{1,0:T(8,128)S(1)} %subtract_select_fusion.2), channel_id=1, source_target_pairs={{0,32},{8,40},{16,48},{24,56},{32,0},{40,8},{48,16},{56,24},{64,96... | collective-permute-start | bytes 2752520 | tf_op jit(solution)/shard_map/ppermute | solution.py:10
  84.0 40.2 %collective-permute-done.2 = f32[256,896]{1,0:T(8,128)S(1)} collective-permute-done((f32[256,896]{1,0:T(8,128)S(1)}, f32[256,896]{1,0:T(8,128)S(1)}, u32[]{:S(2)}, u32[]{:S(2)}) %collective-permute-start.2) | collective-permute-done | bytes 917536 | tf_op jit(solution)/shard_map/ppermute | solution.py:10
  124.2 0.1 subtract_select_fusion.1
  124.3 1.4 collective-permute-start.3
  125.7 19.4 %collective-permute-done.3 = f32[256,896]{1,0:T(8,128)S(1)} collective-permute-done((f32[256,896]{1,0:T(8,128)S(1)}, f32[256,896]{1,0:T(8,128)S(1)}, u32[]{:S(2)}, u32[]{:S(2)}) %collective-permute-start.3) | collective-permute-done | bytes 917536 | tf_op jit(solution)/shard_map/ppermute | solution.py:10
  145.0 0.1 subtract_select_fusion
  145.1 3.0 collective-permute-start.4
  148.2 18.3 %collective-permute-done.4 = f32[256,896]{1,0:T(8,128)S(1)} collective-permute-done((f32[256,896]{1,0:T(8,128)S(1)}, f32[256,896]{1,0:T(8,128)S(1)}, u32[]{:S(2)}, u32[]{:S(2)}) %collective-permute-start.4) | collective-permute-done | bytes 917536 | tf_op jit(solution)/shard_map/ppermute | solution.py:10
  166.4 2.1 fusion
  168.5 0.0 all-gather.2.cloned.1.call-update
  168.5 0.0 reduce-scatter.2.cloned.1.call-start
  168.6 77.4 %all-gather.2.cloned.1.call-done = bf16[240,7168]{1,0:T(8,128)(2,1)} async-done(((bf16[240,896]{1,0:T(8,128)(2,1)}), bf16[240,7168]{1,0:T(8,128)(2,1)}) %all-gather.2.cloned.1.call-update) | async-done | bytes 3440656 | tf_op jit(solution)/shard_map/all_gather | solution.py:48
  246.0 14.6 %fusion.54 = f32[7168,896]{1,0:T(8,128)} fusion(bf16[240,7168]{1,0:T(8,128)(2,1)} %all-gather.2.cloned.1.call-done, bf16[240,896]{1,0:T(8,128)(2,1)} %fusion), kind=kOutput, calls=%fused_computation.159 | convolution fusion | flops 3082813440 | bytes 29560832 | tf_op jit(solution)/shard_map/dot_general | solution.py:50
  260.6 0.0 reduce-scatter.2.cloned.1.call-update
  260.6 1.0 copy-done
  261.6 0.3 convolution_reduce_fusion
  261.9 70.3 %psum.15 = f32[896]{0:T(1024)S(1)} all-reduce(f32[896]{0:T(1024)S(1)} %convolution_reduce_fusion), channel_id=1, replica_groups=mesh['row'=32,'feat'=8] {'row'}, use_global_device_ids=true, to_apply=%region_2.3 | all-reduce | flops 896 | bytes 7168 | tf_op jit(solution)/shard_map/psum | solution.py:36
  332.2 0.6 broadcast_multiply_fusion.1
  332.8 144.2 %reduce-scatter.2.cloned.1.call-done = f32[224,896]{1,0:T(8,128)} async-done(((f32[7168,896]{1,0:T(8,128)}), f32[224,896]{1,0:T(8,128)}) %reduce-scatter.2.cloned.1.call-update) | async-done | bytes 802832 | tf_op jit(solution)/shard_map/reduce_scatter | solution.py:49
  476.9 2.1 broadcast_multiply_fusion
  (9 shorter events, 0.1 us)
Async XLA Ops:
  7.2 238.8 %all-gather.2.cloned.1.call-start = ((), (), s32[]{:S(2)}) async-start(), calls=%async_computation.1 | async-start | bytes 3870720 | tf_op jit(solution)/shard_map/all_gather | solution.py:48
  28.7 6.6 %collective-permute-start = (f32[256,896]{1,0:T(8,128)S(1)}, f32[256,896]{1,0:T(8,128)S(1)}, u32[]{:S(2)}, u32[]{:S(2)}) collective-permute-start(f32[256,896]{1,0:T(8,128)S(1)} %convert_multiply_fusion), channel_id=1, source_target_pairs={{0,8},{8,0},{16,24},{24,16},{32,40},{40,32},{48,56},{56,48},{64,72... | collective-permute-start | bytes 2752520 | tf_op jit(solution)/shard_map/ppermute | solution.py:10
  36.6 41.7 %collective-permute-start.1 = (f32[256,896]{1,0:T(8,128)S(1)}, f32[256,896]{1,0:T(8,128)S(1)}, u32[]{:S(2)}, u32[]{:S(2)}) collective-permute-start(f32[256,896]{1,0:T(8,128)S(1)} %subtract_select_fusion.3), channel_id=1, source_target_pairs={{0,16},{8,24},{16,0},{24,8},{32,48},{40,56},{48,32},{56,40},{64,80... | collective-permute-start | bytes 2752520 | tf_op jit(solution)/shard_map/ppermute | solution.py:10
  78.4 69.7 %copy-start.1 = (s32[240]{0:T(256)S(1)}, s32[240]{0:T(256)}, u32[]{:S(2)}) copy-start(s32[240]{0:T(256)} %param.9) | copy-start | bytes 2884
  78.4 45.8 %collective-permute-start.2 = (f32[256,896]{1,0:T(8,128)S(1)}, f32[256,896]{1,0:T(8,128)S(1)}, u32[]{:S(2)}, u32[]{:S(2)}) collective-permute-start(f32[256,896]{1,0:T(8,128)S(1)} %subtract_select_fusion.2), channel_id=1, source_target_pairs={{0,32},{8,40},{16,48},{24,56},{32,0},{40,8},{48,16},{56,24},{64,96... | collective-permute-start | bytes 2752520 | tf_op jit(solution)/shard_map/ppermute | solution.py:10
  124.3 20.7 %collective-permute-start.3 = (f32[256,896]{1,0:T(8,128)S(1)}, f32[256,896]{1,0:T(8,128)S(1)}, u32[]{:S(2)}, u32[]{:S(2)}) collective-permute-start(f32[256,896]{1,0:T(8,128)S(1)} %subtract_select_fusion.1), channel_id=1, source_target_pairs={{0,64},{8,72},{16,80},{24,88},{32,96},{40,104},{48,112},{56,120},{... | collective-permute-start | bytes 2752520 | tf_op jit(solution)/shard_map/ppermute | solution.py:10
  145.1 21.3 %collective-permute-start.4 = (f32[256,896]{1,0:T(8,128)S(1)}, f32[256,896]{1,0:T(8,128)S(1)}, u32[]{:S(2)}, u32[]{:S(2)}) collective-permute-start(f32[256,896]{1,0:T(8,128)S(1)} %subtract_select_fusion), channel_id=1, source_target_pairs={{0,128},{8,136},{16,144},{24,152},{32,160},{40,168},{48,176},{56,1... | collective-permute-start | bytes 2752520 | tf_op jit(solution)/shard_map/ppermute | solution.py:10
  168.5 308.4 %reduce-scatter.2.cloned.1.call-start = ((), (), s32[]{:S(2)}) async-start(), calls=%async_computation.2 | async-start | bytes 26492928 | tf_op jit(solution)/shard_map/reduce_scatter | solution.py:49
  260.6 1.0 copy-start
Sparse Core Ops, SparseCore 0:
  168.6 77.2 all-gather.1
  260.7 216.1 reduce-scatter.1
where the time goes:
time: 486 us
  waiting for transfers between devices  340 us (70%)
  blocking collectives  87.7 us (18%)
  matrix products  18.4 us (4%)
  starting transfers between devices  17.6 us (4%)
  between operations  14.1 us (3%)
  other arithmetic  6.15 us (1%)
    reduce_scatter x1, waiting for transfers between devices, shards(): lax.psum_scatter(lax.dot_general(whole_sketch, sketch, (((0,), (0,)), (()...  144 us
    ppermute x5, waiting for transfers between devices, swapped(): return lax.ppermute(value, axis, pairs)  119 us
    all_gather x1, waiting for transfers between devices, shards(): whole_sketch = lax.all_gather(sketch, 'feat', axis=1, tiled=True)  77.4 us
    psum x1, blocking collectives, shards(): gradient = lax.psum(grad_term, 'row') / jnp.sqrt(jnp.float32(total_rows))  70.3 us
    ppermute x5, starting transfers between devices, swapped(): return lax.ppermute(value, axis, pairs)  17.5 us
    psum x1, blocking collectives, shards(): logits = lax.psum(partial_logits, 'feat')  17.5 us
    dot_general x1, matrix products, shards(): lax.dot_general(whole_sketch, sketch, (((0,), (0,)), ((), ())), preferred...  14.6 us
  transfers between devices with their start and end apart: 7, of which 7 were waited for; matrix products, arithmetic and copies ran while one was open for 0% of the time, Pallas kernels for 0%

commit v1 on v0

v1 whole, which is shorter than its diff:
```python
import functools

import jax
import jax.numpy as jnp
from jax import lax
from jax.experimental import pallas as pl
from jax.experimental.pallas import tpu as pltpu
from jax.sharding import PartitionSpec as P

BF16, F32, I32 = jnp.bfloat16, jnp.float32, jnp.int32
MESH = pl.DeviceIdType.MESH

NX, NY, NZ, NZC = 4, 4, 8, 8
ROWS = 256
COLS = 896
OUT = 224
HALF = 448
DEPTH = ROWS * NZC
SKIP = 16
SKETCH = 7680
TOTAL = 8192


def nt(a, b):
    return lax.dot_general(a, b, (((1,), (1,)), ((), ())), preferred_element_type=F32)


def nn(a, b):
    return lax.dot_general(a, b, (((1,), (0,)), ((), ())), preferred_element_type=F32)


def split_rows(v):
    hi = v.astype(BF16).astype(F32)
    rest = v - hi
    mid = rest.astype(BF16).astype(F32)
    lo = rest - mid
    rid = lax.broadcasted_iota(I32, (8, v.shape[1]), 0)
    zero = jnp.zeros((8, v.shape[1]), F32)
    rows = jnp.where(rid == 0, hi, jnp.where(rid == 1, mid, jnp.where(rid == 2, lo, zero)))
    return rows.astype(BF16)


def kernel(
    x_ref, w_ref, lab_ref, sgn_ref, smp_ref, gram_ref, grad_ref,
    Z, Y, Ls, Lr, St, Ix, Cs, Cx, Cz, Czr, Cg, CT, Cy, Gb, Gown, Gr, Gs, Grr,
    zs, zr, cs, cr, ys, yr, ls, lr, ss, sr, ia_s, ia_r, ib_s, ib_r,
    cx_s, cx_r, cz_s, cz_r, cg_s, cg_r, cy_s, cy_r, g_s, g_r, d_s, d_r,
):
    row, feat = lax.axis_index("row"), lax.axis_index("feat")
    x, blk = row // NZC, row % NZC
    zh, c = blk // 2, blk % 2
    y, zl = feat // 2, feat % 2
    z = zh * 2 + zl
    q, h = zh // 2, zh % 2

    def dev(x_, z_, c_, y_):
        return (x_ * NZC + (z_ // 2) * 2 + c_, y_ * 2 + z_ % 2)

    def copy(src, dst, ssem, rsem, where):
        return pltpu.make_async_remote_copy(
            src_ref=src, dst_ref=dst, send_sem=ssem, recv_sem=rsem, device_id=where, device_id_type=MESH
        )

    here_other = dev(x, z, 1 - c, y)
    pending = []

    def send(src, dst, ssem, rsem, where):
        cp = copy(src, dst, ssem, rsem, where)
        cp.start()
        pending.append(cp)

    def arrived(dst, rsem):
        copy(dst, dst, rsem, rsem, here_other).wait_recv()

    def column(b):
        return pl.ds(pl.multiple_of(b * ROWS, ROWS), ROWS)

    def zc_dev(b):
        return dev(x, (b // 2) * 2 + zl, b % 2, y)

    Z[zl, :, column(blk)] = x_ref[...].T
    partial = jnp.sum(nt(split_rows(w_ref[...]), x_ref[...]), axis=0, keepdims=True)
    Ls[...] = jnp.broadcast_to(partial, (8, ROWS))
    order = lax.broadcasted_iota(I32, (SKIP, smp_ref.shape[1]), 1)
    rank = lax.broadcasted_iota(I32, (SKIP, smp_ref.shape[1]), 0)
    below = jnp.where(smp_ref[...] - order <= rank, 1.0, 0.0).astype(F32)
    skipped = jnp.sum(below, axis=1, keepdims=True)
    Ix[x, blk] = skipped + lax.broadcasted_iota(I32, (SKIP, 128), 0).astype(F32)

    barrier = pltpu.get_barrier_semaphore()
    greeted = []
    for dz in range(NZ):
        for other in range(2):
            if dz or other:
                greeted.append(dev(x, (z + dz) % NZ, (c + other) % 2, y))
    for dy in range(1, NY):
        greeted.append(dev(x, z, c, (y + dy) % NY))
        greeted.append(dev(x, z, 1 - c, (y + dy) % NY))
        greeted.append(dev(x, zh * 2 + 1 - zl, c, (y + dy) % NY))
    for dx in range(1, NX):
        greeted.append(dev((x + dx) % NX, z, c, y))
    for there in greeted:
        pl.semaphore_signal(barrier, inc=1, device_id=there, device_id_type=MESH)
    pl.semaphore_wait(barrier, len(greeted))

    for d in range(1, 8):
        other = (feat + d) % 8
        send(Ls, Lr.at[d - 1], ls.at[d - 1], lr.at[d - 1], (row, other))
    for d in range(1, NZC):
        b = (blk + d) % NZC
        send(Ix.at[x, blk], Ix.at[x, blk], ia_s.at[d - 1], ia_r.at[d - 1], zc_dev(b))

    def chunk(zsrc, core, j):
        b = (zsrc // 2) * 2 + core
        return Z.at[zsrc % 2, pl.ds(j * HALF, HALF), column(b)]

    def to_ring(i, step, j, zsrc):
        ref = chunk(zsrc, c, j)
        there = dev(x, (z + (1 - 2 * i)) % NZ, c, y)
        send(ref, ref, zs.at[i, step, j], zr.at[i, step, j], there)

    def y_copy(dy, core, zsrc_hi):
        b = zsrc_hi * 2 + c
        start = pl.multiple_of(h * HALF + core * OUT, 32)
        return copy(
            Z.at[q, pl.ds(start, OUT), column(b)],
            Y.at[dy - 1, :, column(b)],
            ys.at[dy - 1, core, zsrc_hi],
            yr.at[dy - 1, b],
            dev(x, z, core, (y + dy) % NY),
        )

    def to_y(zsrc, j):
        wanted = zsrc % 2 == q
        if j is not None:
            wanted = wanted & (h == j)

        @pl.when(wanted)
        def _():
            for dy in (1, 3, 2):
                for core in range(2):
                    y_copy(dy, core, zsrc // 2).start()

    for j in range(2):
        for i in range(2):
            to_ring(i, 0, j, z)
    own = Z.at[zl, :, column(blk)]
    send(own, own, cs.at[0, 4, 0], cr.at[0, 4, 0], here_other)
    to_y(z, None)

    logits = Ls[0:1, :]
    for d in range(1, 8):
        arrived(Lr.at[d - 1], lr.at[d - 1])
        logits = logits + Lr[d - 1, 0:1, :]
    prob = 1.0 / (1.0 + jnp.exp(-logits))
    var = prob * (1.0 - prob)
    resid = prob - lab_ref[...].astype(F32)
    scale = (2 * sgn_ref[...] - 1).astype(F32) * jnp.sqrt(var)
    rid8 = lax.broadcasted_iota(I32, (8, ROWS), 0)
    St[blk] = jnp.where(rid8 == 0, var, resid)
    for d in range(1, NZC):
        b = (blk + d) % NZC
        send(St.at[blk], St.at[blk], ss.at[d - 1], sr.at[d - 1], zc_dev(b))

    for d in range(1, NZC):
        b = (blk + NZC - d) % NZC
        arrived(Ix.at[x, b], ia_r.at[d - 1])
    for dx in range(1, NX):
        send(Ix.at[x], Ix.at[x], ib_s.at[dx - 1], ib_r.at[dx - 1], dev((x + dx) % NX, z, c, y))
    mixed = Z[zl, :, column(blk)].astype(F32) * scale
    mixed_hi = mixed.astype(BF16)
    mixed_lo = (mixed - mixed_hi.astype(F32)).astype(BF16)
    for dx in range(1, NX):
        arrived(Ix.at[(x + NX - dx) % NX], ib_r.at[dx - 1])

    def part_of_plane(plane, carry):
        index = Ix[plane].reshape(NZC * SKIP, 128).astype(I32)
        lane = lax.broadcasted_iota(I32, index.shape, 1)
        block = plane * NZC + lax.broadcasted_iota(I32, index.shape, 0) // SKIP
        low = (index & lane) | ((block & row) << 8)
        signs = []
        for u in (low, low | (index & 128)):
            u = u ^ (u >> 8)
            u = u ^ (u >> 4)
            u = u ^ (u >> 2)
            u = u ^ (u >> 1)
            signs.append((1 - 2 * (u & 1)).astype(F32))
        table = jnp.concatenate(signs, axis=1).astype(BF16)
        Cs[plane] = (nt(table, mixed_hi) + nt(table, mixed_lo)).astype(BF16)
        return carry

    lax.fori_loop(0, NX, part_of_plane, 0)
    for dx in range(1, NX):
        there = (x + dx) % NX
        send(Cs.at[there], Cx.at[dx - 1], cx_s.at[dx - 1], cx_r.at[dx - 1], dev(there, z, c, y))

    def ring_step(step, events):
        for i, j in events:
            zsrc = (z + NZ - (1 - 2 * i) * step) % NZ
            ref = chunk(zsrc, c, j)
            arrived(ref, zr.at[i, step - 1, j])
            if step < 3 or (step == 3 and i == j):
                to_ring(i, step, j, zsrc)
            send(ref, ref, cs.at[i, step - 1, j], cr.at[i, step - 1, j], here_other)
            to_y(zsrc, j)

    both = ((0, 0), (1, 0), (0, 1), (1, 1))
    ring_step(1, both)

    total = Cs[x].astype(F32)
    for dx in range(1, NX):
        arrived(Cx.at[dx - 1], cx_r.at[dx - 1])
        total = total + Cx[dx - 1].astype(F32)
    Cz[...] = total.astype(BF16)

    def sixteen(b):
        return pl.ds(pl.multiple_of(b * SKIP, SKIP), SKIP)

    for d in range(1, NZC):
        b = (blk + d) % NZC
        send(Cz.at[sixteen(b), :], Czr.at[d - 1], cz_s.at[d - 1], cz_r.at[d - 1], zc_dev(b))

    ring_step(2, both)

    total = Cz[sixteen(blk), :].astype(F32)
    for d in range(1, NZC):
        arrived(Czr.at[d - 1], cz_r.at[d - 1])
        total = total + Czr[d - 1].astype(F32)
    Cg[zl, sixteen(blk), :] = total.astype(BF16)
    mine = Cg.at[zl, sixteen(blk), :]
    for dz in range(NZ):
        for other in range(2):
            if dz or other:
                there = dev(x, (z + dz) % NZ, (c + other) % 2, y)
                send(mine, mine, cg_s.at[dz, other], cg_r.at[dz, other], there)

    ring_step(3, both)

    for dz in range(NZ):
        for other in range(2):
            if dz or other:
                zsrc = (z + NZ - dz) % NZ
                b = (zsrc // 2) * 2 + (c + other) % 2
                arrived(Cg.at[zsrc % 2, sixteen(b), :], cg_r.at[dz, other])
    CT[...] = Cg[q].T
    rows_here = pl.ds(pl.multiple_of(h * HALF + c * OUT, 32), OUT)
    for dy in range(1, NY):
        send(CT.at[rows_here, :], Cy.at[dy - 1], cy_s.at[dy - 1], cy_r.at[dy - 1], dev(x, z, c, (y + dy) % NY))

    ring_step(4, ((0, 0), (1, 1)))

    for d in range(1, NZC):
        arrived(St.at[(blk + NZC - d) % NZC], sr.at[d - 1])
    weight = jnp.concatenate([St[b, 0:1, :] for b in range(NZC)], axis=1)
    resids = jnp.concatenate([St[b, 1:2, :] for b in range(NZC)], axis=1)
    own_sib = Z.at[zl, :, column(zh * 2 + 1 - c)]
    arrived(own_sib, cr.at[0, 4, 0])
    for step in range(1, 5):
        for i, j in both if step < 4 else ((0, 0), (1, 1)):
            zsrc = (z + NZ - (1 - 2 * i) * step) % NZ
            arrived(chunk(zsrc, 1 - c, j), cr.at[i, step - 1, j])

    term = jnp.sum(nt(split_rows(resids), Z[zl]), axis=0, keepdims=True)
    Gs[...] = jnp.broadcast_to(term, (8, COLS))
    for dx in range(1, NX):
        send(Gs, Grr.at[dx - 1], d_s.at[dx - 1], d_r.at[dx - 1], dev((x + dx) % NX, z, c, y))

    for dy in (0, 1, 3, 2):
        if dy == 0:
            rows = Z[q, rows_here, :]
            skip = CT[rows_here, :]
        else:
            for b in range(NZC):
                arrived(Y.at[dy - 1, :, column(b)], yr.at[dy - 1, b])
            arrived(Cy.at[dy - 1], cy_r.at[dy - 1])
            rows = Y[dy - 1]
            skip = Cy[dy - 1]
        scaled = rows.astype(F32) * weight
        scaled_hi = scaled.astype(BF16)
        scaled_lo = (scaled - scaled_hi.astype(F32)).astype(BF16)
        block = nt(scaled_hi, Z[zl]) + nt(scaled_lo, Z[zl]) - nn(skip, Cg[zl]) * (1.0 / TOTAL)
        plane = (y + NY - dy) % NY

        @pl.when(plane == x)
        def _():
            Gown[...] = block

        @pl.when(plane != x)
        def _():
            Gb[dy] = block.astype(BF16)
            copy(Gb.at[dy], Gr.at[x], g_s.at[dy], g_r.at[x], dev(plane, z, c, y)).start()

    total = Gs[0:1, :]
    for dx in range(1, NX):
        arrived(Grr.at[dx - 1], d_r.at[dx - 1])
        total = total + Grr[dx - 1, 0:1, :]
    grad_ref[...] = total * (TOTAL ** -0.5)

    total = Gown[...]
    for dx in (1, 3, 2):
        src = (x + dx) % NX
        arrived(Gr.at[src], g_r.at[src])
        total = total + Gr[src].astype(F32)
    gram_ref[...] = total * (SKETCH ** -0.5)

    for cp in pending:
        cp.wait_send()
    for dy in range(1, NY):
        for core in range(2):
            for hi in range(4):
                y_copy(dy, core, hi).wait_send()
    for dy in range(NY):
        plane = (y + NY - dy) % NY

        @pl.when(plane != x)
        def _():
            copy(Gb.at[dy], Gr.at[x], g_s.at[dy], g_r.at[x], dev(plane, z, c, y)).wait_send()


def shards(features, weights, labels, sign_bits, sample_rows):
    vmem = pl.BlockSpec(memory_space=pltpu.VMEM)
    dma = pltpu.SemaphoreType.DMA
    scratch = [
        pltpu.VMEM((2, COLS, DEPTH), BF16),
        pltpu.VMEM((3, OUT, DEPTH), BF16),
        pltpu.VMEM((8, ROWS), F32),
        pltpu.VMEM((7, 8, ROWS), F32),
        pltpu.VMEM((NZC, 8, ROWS), F32),
        pltpu.VMEM((NX, NZC, SKIP, 128), F32),
        pltpu.VMEM((NX, NZC * SKIP, COLS), BF16),
        pltpu.VMEM((3, NZC * SKIP, COLS), BF16),
        pltpu.VMEM((NZC * SKIP, COLS), BF16),
        pltpu.VMEM((7, SKIP, COLS), BF16),
        pltpu.VMEM((2, NZC * SKIP, COLS), BF16),
        pltpu.VMEM((COLS, NZC * SKIP), BF16),
        pltpu.VMEM((3, OUT, NZC * SKIP), BF16),
        pltpu.VMEM((NY, OUT, COLS), BF16),
        pltpu.VMEM((OUT, COLS), F32),
        pltpu.VMEM((NX, OUT, COLS), BF16),
        pltpu.VMEM((8, COLS), F32),
        pltpu.VMEM((3, 8, COLS), F32),
        dma((2, 4, 2)), dma((2, 4, 2)),
        dma((2, 5, 2)), dma((2, 5, 2)),
        dma((3, 2, 4)), dma((3, 8)),
        dma((7,)), dma((7,)),
        dma((7,)), dma((7,)),
        dma((7,)), dma((7,)),
        dma((3,)), dma((3,)),
        dma((3,)), dma((3,)),
        dma((7,)), dma((7,)),
        dma((8, 2)), dma((8, 2)),
        dma((3,)), dma((3,)),
        dma((4,)), dma((4,)),
        dma((3,)), dma((3,)),
    ]
    gram, gradient = pl.pallas_call(
        kernel,
        out_shape=(
            jax.ShapeDtypeStruct((OUT, COLS), F32),
            jax.ShapeDtypeStruct((1, COLS), F32),
        ),
        in_specs=[vmem] * 5,
        out_specs=(vmem, vmem),
        scratch_shapes=scratch,
        compiler_params=pltpu.CompilerParams(
            collective_id=0, has_side_effects=True, vmem_limit_bytes=56 * 2**20
        ),
        name="newton_sketch",
    )(
        features,
        weights.reshape(1, -1),
        labels.reshape(1, -1),
        sign_bits.reshape(1, -1),
        sample_rows.reshape(1, -1),
    )
    return gram, gradient.reshape(-1)


def solution(mesh):
    placed = (P("row", "feat"), P("feat"), P("row"), P("row"), P("row"))
    return jax.shard_map(
        shards, mesh=mesh, in_specs=placed, out_specs=(P("row", "feat"), P("feat")), check_vma=False
    )
```

time: 486 us -> 108 us (0.22)
  waiting for transfers between devices: 340 us -> 0 us
  Pallas kernels: 0 us -> 100 us
  blocking collectives: 87.7 us -> 0 us
  matrix products: 18.4 us -> 0 us
  starting transfers between devices: 17.6 us -> 0 us
  between operations: 14.1 us -> 0.66 us
  other arithmetic: 6.15 us -> 0.61 us
    reduce_scatter x1 -> x0, waiting for transfers between devices: 144 us -> none  [shards(): lax.psum_scatter(lax.dot_general(whole_sketch, sketch, (((0,), (0,)), (()...]
    ppermute x5 -> x0, waiting for transfers between devices: 119 us -> none  [swapped(): return lax.ppermute(value, axis, pairs)]
    pallas_call x0 -> x1, Pallas kernels: none -> 100 us  [shards(): pl.pallas_call(kernel, out_shape=(jax.ShapeDtypeStruct((OUT, COLS), F32),...]
    psum x2 -> x0, blocking collectives: 87.7 us -> none  [the longest x1 70.3 us: shards(): gradient = lax.psum(grad_term, 'row') / jnp.sqrt(jnp.float32(total_rows))]
    all_gather x1 -> x0, waiting for transfers between devices: 77.4 us -> none  [shards(): whole_sketch = lax.all_gather(sketch, 'feat', axis=1, tiled=True)]
    dot_general x4 -> x0, matrix products: 18.4 us -> none  [the longest x1 14.6 us: shards(): lax.dot_general(whole_sketch, sketch, (((0,), (0,)), ((), ())), preferred...]
    ppermute x5 -> x0, starting transfers between devices: 17.5 us -> none  [swapped(): return lax.ppermute(value, axis, pairs)]
  transfers between devices with their start and end apart: 7 -> 0, of which waited for: 7 -> 0; matrix products, arithmetic and copies ran while one was open for 0% -> 0% of each run, Pallas kernels for 0% -> 0%
where the time goes in v1:
time: 108 us; the launch traced here: 105 us
  Pallas kernels  100 us (93%)
  local copies, waits for them, and re-layouts  3.99 us (4%)
    pallas_call x1, Pallas kernels, shards(): pl.pallas_call(kernel, out_shape=(jax.ShapeDtypeStruct((OUT, COLS), F32),...  100 us
    unnamed x5, local copies, waits for them, and re-layouts  3.41 us

profile of v1, /device:TPU:1, one launch (start us, length us, event | category | flops | bytes accessed | tf_op | source)
XLA Modules:
  0.0 105.5 jit_solution(17294408853898654218)
XLA Ops:
  0.6 0.0 copy-start
  0.6 0.7 copy-done
  1.3 0.6 reshape.19.w_ref
  1.9 100.2 %newton_sketch.1 = (f32[224,896]{1,0:T(8,128)}, f32[1,896]{1,0:T(1,128)}) custom-call(bf16[256,896]{1,0:T(8,128)(2,1)} %x_ref.1, f32[1,896]{1,0:T(1,128)} %reshape.19.w_ref, s32[1,256]{1,0:T(1,128)} %bitcast.3, s32[1,256]{1,0:T(1,128)} %bitcast.4, s32[1,240]{1,0:T(1,128)} %bitcast.5), custom_call_target="tpu_custom_call" | custom-call | tf_op jit(solution)/shard_map/newton_sketch/pallas_call | solution.py:356
  102.1 0.0 copy-start.1
  102.1 0.7 copy-done.1
  102.8 0.6 reduce
  103.4 2.1 %copy.8 = f32[224,896]{1,0:T(8,128)} copy(f32[224,896]{1,0:T(8,128)} %get-tuple-element.8) | data formatting | bytes 1605632
Async XLA Ops:
  0.6 0.7 copy-start
  102.1 0.7 copy-start.1

commit v2 on v0

v2 whole, which is shorter than its diff:
```python
import functools

import jax
import jax.numpy as jnp
from jax import lax
from jax.experimental import pallas as pl
from jax.experimental.pallas import tpu as pltpu
from jax.sharding import PartitionSpec as P

BF16, F32, I32 = jnp.bfloat16, jnp.float32, jnp.int32
MESH = pl.DeviceIdType.MESH

NX, NY, NZ, NZC = 4, 4, 8, 8
ROWS = 256
COLS = 896
OUT = 224
PART = (160, 64)
OFF = (0, 160)
BASE = (0, 640)
DEPTH = ROWS * NZC
SKIP = 16
SKETCH = 7680
TOTAL = 8192


def nt(a, b):
    return lax.dot_general(a, b, (((1,), (1,)), ((), ())), preferred_element_type=F32)


def nn(a, b):
    return lax.dot_general(a, b, (((1,), (0,)), ((), ())), preferred_element_type=F32)


def split_rows(v):
    hi = v.astype(BF16).astype(F32)
    rest = v - hi
    mid = rest.astype(BF16).astype(F32)
    lo = rest - mid
    rid = lax.broadcasted_iota(I32, (8, v.shape[1]), 0)
    zero = jnp.zeros((8, v.shape[1]), F32)
    rows = jnp.where(rid == 0, hi, jnp.where(rid == 1, mid, jnp.where(rid == 2, lo, zero)))
    return rows.astype(BF16)


def kernel(
    x_ref, w_ref, lab_ref, sgn_ref, smp_ref, gram_ref, grad_ref,
    Z, Y, Ls, Lr, St, Ix, Tb, Cs, Cx, Cg, CT, Cy, Gm, Gb, Gown, Gr, Gs, Grr,
    zs, zr, cs, cr, ys, yr, yf, ls, lr, ss, sr, ia_s, ia_r, ib_s, ib_r,
    cx_s, cx_r, cg_s, cg_r, cy_r, cp_s, g_s, g_r, d_s, d_r,
):
    row, feat = lax.axis_index("row"), lax.axis_index("feat")
    x, blk = row // NZC, row % NZC
    zh, c = blk // 2, blk % 2
    y, zl = feat // 2, feat % 2
    z = zh * 2 + zl
    q, h = zh // 2, zh % 2

    def dev(x_, z_, c_, y_):
        return (x_ * NZC + (z_ // 2) * 2 + c_, y_ * 2 + z_ % 2)

    here_other = dev(x, z, 1 - c, y)

    def zc_dev(b):
        return dev(x, (b // 2) * 2 + zl, b % 2, y)

    barrier = pltpu.get_barrier_semaphore()
    greeted = [zc_dev((blk + d) % NZC) for d in range(1, NZC)]
    greeted += [dev(x, (z + 1) % NZ, c, y), dev(x, (z + NZ - 1) % NZ, c, y)]
    for dy in range(1, NY):
        greeted.append(dev(x, z, c, (y + dy) % NY))
        greeted.append(dev(x, z, 1 - c, (y + dy) % NY))
        greeted.append(dev(x, zh * 2 + 1 - zl, c, (y + dy) % NY))
    for dx in range(1, NX):
        greeted.append(dev((x + dx) % NX, z, c, y))
    for there in greeted:
        pl.semaphore_signal(barrier, inc=1, device_id=there, device_id_type=MESH)

    def copy(src, dst, ssem, rsem, where):
        return pltpu.make_async_remote_copy(
            src_ref=src, dst_ref=dst, send_sem=ssem, recv_sem=rsem, device_id=where, device_id_type=MESH
        )

    pending = []

    def send(src, dst, ssem, rsem, where):
        cp = copy(src, dst, ssem, rsem, where)
        cp.start()
        pending.append(cp)

    def arrived(dst, rsem):
        copy(dst, dst, rsem, rsem, here_other).wait_recv()

    def column(b):
        return pl.ds(pl.multiple_of(b * ROWS, ROWS), ROWS)

    turned = x_ref[...].T
    for p in range(2):
        for g in range(4):
            Z[zl, pl.ds(BASE[p] + g * PART[p], PART[p]), column(blk)] = turned[
                g * OUT + OFF[p] : g * OUT + OFF[p] + PART[p]
            ]
    partial = jnp.sum(nt(split_rows(w_ref[...].reshape(1, COLS)), x_ref[...]), axis=0, keepdims=True)
    Ls[...] = jnp.broadcast_to(partial, (8, ROWS))
    order = lax.broadcasted_iota(I32, (SKIP, smp_ref.shape[0]), 1)
    rank = lax.broadcasted_iota(I32, (SKIP, smp_ref.shape[0]), 0)
    below = jnp.where(smp_ref[...].reshape(1, -1) - order <= rank, 1.0, 0.0).astype(F32)
    skipped = jnp.sum(below, axis=1, keepdims=True)
    Ix[x, blk] = skipped + lax.broadcasted_iota(I32, (SKIP, 128), 0).astype(F32)

    pl.semaphore_wait(barrier, len(greeted))

    for d in range(1, 8):
        send(Ls, Lr.at[d - 1], ls.at[d - 1], lr.at[d - 1], (row, (feat + d) % 8))
    for d in range(1, NZC):
        mine = Ix.at[x, blk]
        send(mine, mine, ia_s.at[d - 1], ia_r.at[d - 1], zc_dev((blk + d) % NZC))

    def chunk(zsrc, core, p, j):
        b = (zsrc // 2) * 2 + core
        return Z.at[zsrc % 2, pl.ds(BASE[p] + 2 * j * PART[p], 2 * PART[p]), column(b)]

    def to_ring(p, i, step, j, zsrc):
        ref = chunk(zsrc, c, p, j)
        there = dev(x, (z + (1 - 2 * i)) % NZ, c, y)
        send(ref, ref, zs.at[p, i, step, j], zr.at[p, i, step, j], there)

    def gram_rows(p, core):
        start = pl.multiple_of(BASE[p] + (2 * h + core) * PART[p], 32)
        return pl.ds(start, PART[p])

    def kept(p):
        return pl.ds(OFF[p], PART[p])

    def y_copy(p, way, core, zsrc_hi):
        dy = (1, 3)[way]
        b = zsrc_hi * 2 + c
        return copy(
            Z.at[q, gram_rows(p, core), column(b)],
            Y.at[dy - 1, kept(p), column(b)],
            ys.at[p, way, core, zsrc_hi],
            yr.at[p, dy - 1, b],
            dev(x, z, core, (y + dy) % NY),
        )

    def to_y(p, zsrc, j):
        wanted = zsrc % 2 == q
        if j is not None:
            wanted = wanted & (h == j)

        @pl.when(wanted)
        def _():
            for way in range(2):
                for core in range(2):
                    y_copy(p, way, core, zsrc // 2).start()

    sg = 1 - 2 * h
    pieces = [
        (jnp.where(q == zl, z + a, z + b) + NZ) % NZ
        for a, b in ((0, -sg), (-2 * sg, sg), (2 * sg, -3 * sg), (4, 3 * sg))
    ]

    def y_forward(p, k):
        for way in range(2):
            b = (pieces[k] // 2) * 2 + way
            slot = 2 * way
            ref = Y.at[slot, kept(p), column(b)]
            arrived(ref, yr.at[p, slot, b])
            there = dev(x, z, c, (y + (1, 3)[way]) % NY)
            send(ref, Y.at[1, kept(p), column(b)], yf.at[p, way, k], yr.at[p, 1, b], there)

    def ring_start(p):
        for jj in range(2):
            for i in range(2):
                to_ring(p, i, 0, jj if i == 0 else 1 - jj, z)
        own = Z.at[zl, pl.ds(BASE[p], 4 * PART[p]), column(blk)]
        send(own, own, cs.at[p, 0, 4, 0], cr.at[p, 0, 4, 0], here_other)
        to_y(p, z, None)

    def ring_event(p, step, jj):
        for i in range(2):
            j = jj if i == 0 else 1 - jj
            zsrc = (z + NZ - (1 - 2 * i) * step) % NZ
            ref = chunk(zsrc, c, p, j)
            arrived(ref, zr.at[p, i, step - 1, j])
            if step < 3 or (step == 3 and jj == 0):
                to_ring(p, i, step, j, zsrc)
            send(ref, ref, cs.at[p, i, step - 1, j], cr.at[p, i, step - 1, j], here_other)
            to_y(p, zsrc, j)

    def sibling_arrived(p):
        own = Z.at[zl, pl.ds(BASE[p], 4 * PART[p]), column(zh * 2 + 1 - c)]
        arrived(own, cr.at[p, 0, 4, 0])
        for step in range(1, 5):
            for jj in range(2 if step < 4 else 1):
                for i in range(2):
                    j = jj if i == 0 else 1 - jj
                    zsrc = (z + NZ - (1 - 2 * i) * step) % NZ
                    arrived(chunk(zsrc, 1 - c, p, j), cr.at[p, i, step - 1, j])

    ring_start(0)

    logits = Ls[0:1, :]
    for d in range(1, 8):
        arrived(Lr.at[d - 1], lr.at[d - 1])
        logits = logits + Lr[d - 1, 0:1, :]
    prob = 1.0 / (1.0 + jnp.exp(-logits))
    var = prob * (1.0 - prob)
    resid = prob - lab_ref[...].reshape(1, ROWS).astype(F32)
    scale = (2 * sgn_ref[...].reshape(1, ROWS) - 1).astype(F32) * jnp.sqrt(var)
    rid8 = lax.broadcasted_iota(I32, (8, ROWS), 0)
    St[blk] = jnp.where(rid8 == 0, var, jnp.where(rid8 == 1, resid, scale))
    for d in range(1, NZC):
        send(St.at[blk], St.at[blk], ss.at[d - 1], sr.at[d - 1], zc_dev((blk + d) % NZC))

    ring_event(0, 1, 0)

    for d in range(1, NZC):
        arrived(Ix.at[x, (blk + NZC - d) % NZC], ia_r.at[d - 1])
    for dx in range(1, NX):
        send(Ix.at[x], Ix.at[x], ib_s.at[dx - 1], ib_r.at[dx - 1], dev((x + dx) % NX, z, c, y))

    ring_event(0, 1, 1)
    ring_event(0, 2, 0)
    y_forward(0, 0)

    for dx in range(1, NX):
        arrived(Ix.at[(x + NX - dx) % NX], ib_r.at[dx - 1])
    index = jnp.concatenate([Ix[u, 2 * v + c] for u in range(NX) for v in range(4)], axis=0).astype(I32)
    lane = lax.broadcasted_iota(I32, index.shape, 1)
    place = lax.broadcasted_iota(I32, index.shape, 0) // SKIP
    block = (place // 4) * NZC + (place % 4) * 2 + c

    def parity(u):
        u = u ^ (u >> 8)
        u = u ^ (u >> 4)
        u = u ^ (u >> 2)
        u = u ^ (u >> 1)
        return u & 1

    low = parity(index & lane)
    high = low ^ ((index >> 7) & 1)
    for b in range(NZC):
        flip = parity(block & (x * NZC + b))
        for part, bits in enumerate((low, high)):
            Tb[:, b * ROWS + part * 128 : b * ROWS + part * 128 + 128] = (1 - 2 * (bits ^ flip)).astype(F32).astype(BF16)

    ring_event(0, 2, 1)
    ring_event(0, 3, 0)
    y_forward(0, 1)
    ring_event(0, 3, 1)
    ring_start(1)

    for d in range(1, NZC):
        arrived(St.at[(blk + NZC - d) % NZC], sr.at[d - 1])
    weight = jnp.concatenate([St[b, 0:1, :] for b in range(NZC)], axis=1)
    resids = jnp.concatenate([St[b, 1:2, :] for b in range(NZC)], axis=1)
    scales = jnp.concatenate([St[b, 2:3, :] for b in range(NZC)], axis=1)

    def out_copy(dy, p, shape):
        plane = (y + NY - dy) % NY
        if shape == 0:
            where = (pl.ds(0, OFF[p]), pl.ds(BASE[p], 4 * PART[p]))
        else:
            where = (kept(p), pl.ds(0, BASE[p] + 4 * PART[p]))
        return copy(
            Gb.at[(dy,) + where], Gr.at[(x,) + where],
            g_s.at[dy, p, shape], g_r.at[x, p, shape], dev(plane, z, c, y),
        )

    def pieces_of(p, shape):
        if shape == 0:
            return tuple(range(p)), pl.ds(BASE[p], 4 * PART[p])
        return (p,), pl.ds(0, BASE[p] + 4 * PART[p])

    def product(dy, p, shape):
        parts, cols = pieces_of(p, shape)
        for r in parts:
            rows = Z[q, gram_rows(r, c), :] if dy == 0 else Y[dy - 1, kept(r), :]
            scaled = rows.astype(F32) * weight
            scaled_hi = scaled.astype(BF16)
            scaled_lo = (scaled - scaled_hi.astype(F32)).astype(BF16)
            both = nt(jnp.concatenate([scaled_hi, scaled_lo], axis=0), Z[zl, cols, :])
            Gm[dy, kept(r), cols] = both[: PART[r]] + both[PART[r] :]

    def finish(dy, p, shape):
        parts, cols = pieces_of(p, shape)
        plane = (y + NY - dy) % NY
        for r in parts:
            block = Gm[dy, kept(r), cols] - nn(Cy[dy, kept(r), :], Cg[:, cols]) * (1.0 / TOTAL)

            @pl.when(plane == x)
            def _():
                Gown[kept(r), cols] = block

            @pl.when(plane != x)
            def _():
                Gb[dy, kept(r), cols] = block.astype(BF16)

        @pl.when(plane != x)
        def _():
            out_copy(dy, p, shape).start()

    def y_arrived(p, dy):
        for b in range(NZC):
            if dy == 2 or b % 2 == (1 if dy == 1 else 0):
                arrived(Y.at[dy - 1, kept(p), column(b)], yr.at[p, dy - 1, b])

    def features(p):
        return pl.ds(BASE[p], 4 * PART[p])

    def half_rows(core):
        return pl.ds(pl.multiple_of(core * 4 * SKIP, 4 * SKIP), 4 * SKIP)

    def plane_rows(u):
        return pl.ds(pl.multiple_of(u * 4 * SKIP, 4 * SKIP), 4 * SKIP)

    def skipped_part(p):
        mixed = (Z[zl, features(p), :].astype(F32) * scales).astype(BF16)
        Cs[:, features(p)] = nt(Tb[...], mixed).astype(BF16)
        for dx in (2, 1, 3):
            there = (x + dx) % NX
            send(
                Cs.at[plane_rows(there), features(p)], Cx.at[dx - 1, :, features(p)],
                cx_s.at[p, dx - 1], cx_r.at[p, dx - 1], dev(there, z, c, y),
            )

    def skipped_sum(p):
        total = Cs[plane_rows(x), features(p)].astype(F32)
        for dx in range(1, NX):
            arrived(Cx.at[dx - 1, :, features(p)], cx_r.at[p, dx - 1])
            total = total + Cx[dx - 1, :, features(p)].astype(F32)
        mine = Cg.at[half_rows(c), features(p)]
        mine[...] = total.astype(BF16)
        send(mine, mine, cg_s.at[p], cg_r.at[p], here_other)

    def c_copy(p, dy, far):
        there = dev(x, zh * 2 + (1 - zl if far else zl), c, (y + dy) % NY)
        return copy(
            CT.at[gram_rows(p, c), :], Cy.at[dy, kept(p), :], cp_s.at[p, dy, far], cy_r.at[p, dy], there
        )

    c_targets = [(dy, far) for dy in (1, 3, 2, 0) for far in range(2) if dy or far]

    def skipped_spread(p):
        arrived(Cg.at[half_rows(1 - c), features(p)], cg_r.at[p])

        @pl.when(q == zl)
        def _():
            CT[features(p), :] = Cg[:, features(p)].T
            for dy, far in c_targets:
                c_copy(p, dy, far).start()
            Cy[0, kept(p), :] = CT[gram_rows(p, c), :]

    def skipped_arrived(p, dy):
        if dy:
            arrived(Cy.at[dy, kept(p), :], cy_r.at[p, dy])
        else:

            @pl.when(q != zl)
            def _():
                arrived(Cy.at[dy, kept(p), :], cy_r.at[p, dy])

    ring_event(0, 4, 0)
    y_forward(0, 2)
    sibling_arrived(0)
    skipped_part(0)
    ring_event(1, 1, 0)
    ring_event(1, 1, 1)
    product(0, 0, 1)
    ring_event(1, 2, 0)
    y_forward(0, 3)
    ring_event(1, 2, 1)
    skipped_sum(0)
    ring_event(1, 3, 0)
    y_forward(1, 0)
    y_arrived(0, 1)
    product(1, 0, 1)
    ring_event(1, 3, 1)
    skipped_spread(0)
    y_forward(1, 1)
    y_arrived(0, 3)
    product(3, 0, 1)
    ring_event(1, 4, 0)
    sibling_arrived(1)
    skipped_part(1)
    y_forward(1, 2)
    skipped_arrived(0, 0)
    finish(0, 0, 1)
    y_forward(1, 3)
    y_arrived(0, 2)
    product(2, 0, 1)
    for dy in (1, 3, 2):
        skipped_arrived(0, dy)
        finish(dy, 0, 1)
    skipped_sum(1)
    term = jnp.sum(nt(split_rows(resids), Z[zl]), axis=0, keepdims=True)
    Gs[...] = jnp.broadcast_to(term, (8, COLS))
    for dx in range(1, NX):
        send(Gs, Grr.at[dx - 1], d_s.at[dx - 1], d_r.at[dx - 1], dev((x + dx) % NX, z, c, y))
    product(0, 1, 0)
    skipped_spread(1)
    finish(0, 1, 0)
    for dy in (1, 3, 2):
        product(dy, 1, 0)
        finish(dy, 1, 0)
    product(0, 1, 1)
    skipped_arrived(1, 0)
    finish(0, 1, 1)
    for dy in (1, 3, 2):
        y_arrived(1, dy)
        product(dy, 1, 1)
        skipped_arrived(1, dy)
        finish(dy, 1, 1)

    def natural(v):
        cuts = []
        for g in range(4):
            for p in range(2):
                start = BASE[p] + g * PART[p]
                cuts.append(v[:, start : start + PART[p]])
        return jnp.concatenate(cuts, axis=1)

    total = Gs[...]
    for dx in range(1, NX):
        arrived(Grr.at[dx - 1], d_r.at[dx - 1])
        total = total + Grr[dx - 1]
    grad_ref[...] = (natural(total)[0:1, :] * (TOTAL ** -0.5)).reshape(COLS)

    for dx in (1, 3, 2):
        src = (x + dx) % NX
        for p, shape in ((0, 1), (1, 0), (1, 1)):
            if shape == 0:
                where = (pl.ds(0, OFF[p]), pl.ds(BASE[p], 4 * PART[p]))
            else:
                where = (kept(p), pl.ds(0, BASE[p] + 4 * PART[p]))
            arrived(Gr.at[(src,) + where], g_r.at[src, p, shape])
    total = Gown[...]
    for dx in range(1, NX):
        total = total + Gr[(x + dx) % NX].astype(F32)
    gram_ref[...] = natural(total) * (SKETCH ** -0.5)

    for cp in pending:
        cp.wait_send()
    for p in range(2):
        for way in range(2):
            for core in range(2):
                for hi in range(4):
                    y_copy(p, way, core, hi).wait_send()
    @pl.when(q == zl)
    def _():
        for p in range(2):
            for dy, far in c_targets:
                c_copy(p, dy, far).wait_send()

    for dy in range(NY):

        @pl.when((y + NY - dy) % NY != x)
        def _():
            for p, shape in ((0, 1), (1, 0), (1, 1)):
                out_copy(dy, p, shape).wait_send()


def shards(features, weights, labels, sign_bits, sample_rows):
    vmem = pl.BlockSpec(memory_space=pltpu.VMEM)
    dma = pltpu.SemaphoreType.DMA
    scratch = [
        pltpu.VMEM((2, COLS, DEPTH), BF16),
        pltpu.VMEM((3, OUT, DEPTH), BF16),
        pltpu.VMEM((8, ROWS), F32),
        pltpu.VMEM((7, 8, ROWS), F32),
        pltpu.VMEM((NZC, 8, ROWS), F32),
        pltpu.VMEM((NX, NZC, SKIP, 128), F32),
        pltpu.VMEM((NX * 4 * SKIP, DEPTH), BF16),
        pltpu.VMEM((NX * 4 * SKIP, COLS), BF16),
        pltpu.VMEM((3, 4 * SKIP, COLS), BF16),
        pltpu.VMEM((NZC * SKIP, COLS), BF16),
        pltpu.VMEM((COLS, NZC * SKIP), BF16),
        pltpu.VMEM((NY, OUT, NZC * SKIP), BF16),
        pltpu.VMEM((NY, OUT, COLS), F32),
        pltpu.VMEM((NY, OUT, COLS), BF16),
        pltpu.VMEM((OUT, COLS), F32),
        pltpu.VMEM((NX, OUT, COLS), BF16),
        pltpu.VMEM((8, COLS), F32),
        pltpu.VMEM((3, 8, COLS), F32),
        dma((2, 2, 4, 2)), dma((2, 2, 4, 2)),
        dma((2, 2, 5, 2)), dma((2, 2, 5, 2)),
        dma((2, 2, 2, 4)), dma((2, 3, 8)), dma((2, 2, 4)),
        dma((7,)), dma((7,)),
        dma((7,)), dma((7,)),
        dma((7,)), dma((7,)),
        dma((3,)), dma((3,)),
        dma((2, 3)), dma((2, 3)),
        dma((2,)), dma((2,)),
        dma((2, 4)), dma((2, 4, 2)),
        dma((4, 2, 2)), dma((4, 2, 2)),
        dma((3,)), dma((3,)),
    ]
    gram, gradient = pl.pallas_call(
        kernel,
        out_shape=(
            jax.ShapeDtypeStruct((OUT, COLS), F32),
            jax.ShapeDtypeStruct((COLS,), F32),
        ),
        in_specs=[vmem] * 5,
        out_specs=(vmem, vmem),
        scratch_shapes=scratch,
        compiler_params=pltpu.CompilerParams(
            collective_id=0, has_side_effects=True, vmem_limit_bytes=56 * 2**20
        ),
        name="newton_sketch",
    )(
        features, weights, labels, sign_bits, sample_rows
    )
    return gram, gradient


def solution(mesh):
    placed = (P("row", "feat"), P("feat"), P("row"), P("row"), P("row"))
    return jax.shard_map(
        shards, mesh=mesh, in_specs=placed, out_specs=(P("row", "feat"), P("feat")), check_vma=False
    )
```

time: 486 us -> 88.9 us (0.18)
  the two profiles are of different devices: /device:TPU:1 before, /device:TPU:17 now
where the time goes in v2:
time: 88.9 us; the launch traced here: 88.8 us
  Pallas kernels  85.5 us (96%)
  local copies, waits for them, and re-layouts  2.67 us (3%)
    pallas_call x1, Pallas kernels, shards(): pl.pallas_call(kernel, out_shape=(jax.ShapeDtypeStruct((OUT, COLS), F32),...  85.5 us
    unnamed x4, local copies, waits for them, and re-layouts  2.67 us

profile of v2, /device:TPU:17, one launch (start us, length us, event | category | flops | bytes accessed | tf_op | source)
XLA Modules:
  0.0 88.8 jit_solution(1467456731882459377)
XLA Ops:
  0.6 85.5 %newton_sketch.1 = (f32[224,896]{1,0:T(8,128)}, f32[896]{0:T(1024)}) custom-call(bf16[256,896]{1,0:T(8,128)(2,1)} %x_ref.1, f32[896]{0:T(1024)} %w_ref.1, s32[256]{0:T(256)} %lab_ref.1, s32[256]{0:T(256)} %sgn_ref.1, s32[240]{0:T(256)} %smp_ref.1), custom_call_target="tpu_custom_call" | custom-call | tf_op jit(solution)/shard_map/newton_sketch/pallas_call | solution.py:498
  86.1 0.0 copy-start
  86.1 2.1 %copy.9 = f32[224,896]{1,0:T(8,128)} copy(f32[224,896]{1,0:T(8,128)} %get-tuple-element.4) | data formatting | bytes 1605632
  88.2 0.0 copy-done
  88.2 0.6 copy.10
Async XLA Ops:
  86.1 2.1 %copy-start = (f32[896]{0:T(1024)S(1)}, f32[896]{0:T(1024)}, u32[]{:S(2)}) copy-start(f32[896]{0:T(1024)} %get-tuple-element.5) | copy-start | bytes 10756

commit v3 on v2

v3 whole, which is shorter than its diff:
```python
import functools

import jax
import jax.numpy as jnp
from jax import lax
from jax.experimental import pallas as pl
from jax.experimental.pallas import tpu as pltpu
from jax.sharding import PartitionSpec as P

BF16, F32, I32 = jnp.bfloat16, jnp.float32, jnp.int32
MESH = pl.DeviceIdType.MESH

NX, NY, NZ, NZC = 4, 4, 8, 8
ROWS = 256
COLS = 896
OUT = 224
PART = (128, 96)
OFF = (0, 128)
BASE = (0, 512)
DEPTH = ROWS * NZC
SKIP = 16
SKETCH = 7680
TOTAL = 8192
TABLE = 256
HEAD = TABLE + 16


def nt(a, b):
    return lax.dot_general(a, b, (((1,), (1,)), ((), ())), preferred_element_type=F32)


def nn(a, b):
    return lax.dot_general(a, b, (((1,), (0,)), ((), ())), preferred_element_type=F32)


def split_rows(v):
    hi = v.astype(BF16).astype(F32)
    rest = v - hi
    mid = rest.astype(BF16).astype(F32)
    lo = rest - mid
    rid = lax.broadcasted_iota(I32, (16, v.shape[1]), 0)
    zero = jnp.zeros((16, v.shape[1]), F32)
    rows = jnp.where(rid == 0, hi, jnp.where(rid == 1, mid, jnp.where(rid == 2, lo, zero)))
    return rows.astype(BF16)


def kernel(
    x_ref, w_ref, lab_ref, sgn_ref, smp_ref, gram_ref, grad_ref,
    Z, Y, Ls, Lr, St, Ix, La, Lb, Cs, Cx, Cg, CT, Cy, Gm, Gb, Gown, Gr, Gs, Grr,
    zs, zr, cs, cr, ys, yr, y2, yf, ls, lr, ss, sr, ia_s, ia_r, ib_s, ib_r,
    cx_s, cx_r, cg_s, cg_r, cy_r, cy_s, g_s, g_r, d_s, d_r,
):
    row, feat = lax.axis_index("row"), lax.axis_index("feat")
    x, blk = row // NZC, row % NZC
    zh, c = blk // 2, blk % 2
    y, zl = feat // 2, feat % 2
    z = zh * 2 + zl
    q, h = zh // 2, zh % 2

    def dev(x_, z_, c_, y_):
        return (x_ * NZC + (z_ // 2) * 2 + c_, y_ * 2 + z_ % 2)

    here_other = dev(x, z, 1 - c, y)

    def zc_dev(b):
        return dev(x, (b // 2) * 2 + zl, b % 2, y)

    barrier = pltpu.get_barrier_semaphore()
    greeted = [zc_dev((blk + d) % NZC) for d in range(1, NZC)]
    greeted += [dev(x, (z + 1) % NZ, c, y), dev(x, (z + NZ - 1) % NZ, c, y)]
    for dy in range(1, NY):
        greeted.append(dev(x, z, c, (y + dy) % NY))
        greeted.append(dev(x, z, 1 - c, (y + dy) % NY))
        greeted.append(dev(x, zh * 2 + 1 - zl, c, (y + dy) % NY))
    for dx in range(1, NX):
        greeted.append(dev((x + dx) % NX, z, c, y))
    for there in greeted:
        pl.semaphore_signal(barrier, inc=1, device_id=there, device_id_type=MESH)

    def copy(src, dst, ssem, rsem, where):
        return pltpu.make_async_remote_copy(
            src_ref=src, dst_ref=dst, send_sem=ssem, recv_sem=rsem, device_id=where, device_id_type=MESH
        )

    def send(src, dst, ssem, rsem, where):
        copy(src, dst, ssem, rsem, where).start()

    def arrived(dst, rsem):
        copy(dst, dst, rsem, rsem, here_other).wait_recv()

    def departed(src, ssem):
        copy(src, src, ssem, ssem, here_other).wait_send()

    def column(b):
        return pl.ds(pl.multiple_of(b * ROWS, ROWS), ROWS)

    turned = x_ref[...].T
    for p in range(2):
        for g in range(4):
            Z[zl, pl.ds(BASE[p] + g * PART[p], PART[p]), column(blk)] = turned[
                g * OUT + OFF[p] : g * OUT + OFF[p] + PART[p]
            ]
    partial = jnp.sum(nt(split_rows(w_ref[...].reshape(1, COLS)), x_ref[...]), axis=0, keepdims=True)
    Ls[...] = jnp.broadcast_to(partial, (8, ROWS))
    order = lax.broadcasted_iota(I32, (SKIP, smp_ref.shape[0]), 1)
    rank = lax.broadcasted_iota(I32, (SKIP, smp_ref.shape[0]), 0)
    below = jnp.where(smp_ref[...].reshape(1, -1) - order <= rank, 1.0, 0.0).astype(F32)
    skipped = jnp.sum(below, axis=1, keepdims=True)
    Ix[x, blk] = skipped + lax.broadcasted_iota(I32, (SKIP, 128), 0).astype(F32)

    pl.semaphore_wait(barrier, len(greeted))

    for d in range(1, 8):
        send(Ls, Lr.at[d - 1], ls.at[0], lr.at[0], (row, (feat + d) % 8))
    for d in range(1, NZC):
        mine = Ix.at[x, blk]
        send(mine, mine, ia_s.at[0], ia_r.at[0], zc_dev((blk + d) % NZC))

    def chunk(zsrc, core, p, j):
        b = (zsrc // 2) * 2 + core
        return Z.at[zsrc % 2, pl.ds(BASE[p] + 2 * j * PART[p], 2 * PART[p]), column(b)]

    def to_ring(p, i, step, j, zsrc):
        ref = chunk(zsrc, c, p, j)
        there = dev(x, (z + (1 - 2 * i)) % NZ, c, y)
        send(ref, ref, zs.at[p], zr.at[p, i, step, j], there)

    def gram_rows(p, core):
        start = pl.multiple_of(BASE[p] + (2 * h + core) * PART[p], 32)
        return pl.ds(start, PART[p])

    def kept(p):
        return pl.ds(OFF[p], PART[p])

    def y_copy(p, way, core, zsrc_hi):
        dy = (1, 3)[way]
        b = zsrc_hi * 2 + c
        return copy(
            Z.at[q, gram_rows(p, core), column(b)],
            Y.at[dy - 1, kept(p), column(b)],
            ys.at[p],
            yr.at[p, way, jnp.where(c == way, zsrc_hi, 4)],
            dev(x, z, core, (y + dy) % NY),
        )

    def to_y(p, zsrc, j):
        wanted = zsrc % 2 == q
        if j is not None:
            wanted = wanted & (h == j)

        @pl.when(wanted)
        def _():
            for way in range(2):
                for core in range(2):
                    y_copy(p, way, core, zsrc // 2).start()

    sg = 1 - 2 * h
    pieces = [
        (jnp.where(q == zl, z + a, z + b) + NZ) % NZ
        for a, b in ((0, -sg), (-2 * sg, sg), (2 * sg, -3 * sg), (4, 3 * sg))
    ]

    def y_forward(p, k):
        for way in range(2):
            b = (pieces[k] // 2) * 2 + way
            slot = 2 * way
            ref = Y.at[slot, kept(p), column(b)]
            arrived(ref, yr.at[p, way, pieces[k] // 2])
            there = dev(x, z, c, (y + (1, 3)[way]) % NY)
            send(ref, Y.at[1, kept(p), column(b)], yf.at[p], y2.at[p], there)

    def ring_start(p):
        for jj in range(2):
            for i in range(2):
                to_ring(p, i, 0, jj if i == 0 else 1 - jj, z)
        own = Z.at[zl, pl.ds(BASE[p], 4 * PART[p]), column(blk)]
        send(own, own, cs.at[p], cr.at[p], here_other)
        to_y(p, z, None)

    def ring_event(p, step, jj):
        for i in range(2):
            j = jj if i == 0 else 1 - jj
            zsrc = (z + NZ - (1 - 2 * i) * step) % NZ
            ref = chunk(zsrc, c, p, j)
            arrived(ref, zr.at[p, i, step - 1, j])
            if step < 3 or (step == 3 and jj == 0):
                to_ring(p, i, step, j, zsrc)
            send(ref, ref, cs.at[p], cr.at[p], here_other)
            to_y(p, zsrc, j)

    def sibling_arrived(p):
        arrived(Z.at[zl, pl.ds(BASE[p], 4 * PART[p]), :], cr.at[p])

    ring_start(0)

    logits = Ls[0:1, :]
    arrived(Lr, lr.at[0])
    for d in range(1, 8):
        logits = logits + Lr[d - 1, 0:1, :]
    prob = 1.0 / (1.0 + jnp.exp(-logits))
    var = prob * (1.0 - prob)
    resid = prob - lab_ref[...].reshape(1, ROWS).astype(F32)
    scale = (2 * sgn_ref[...].reshape(1, ROWS) - 1).astype(F32) * jnp.sqrt(var)
    rid8 = lax.broadcasted_iota(I32, (8, ROWS), 0)
    St[blk] = jnp.where(rid8 == 0, var, jnp.where(rid8 == 1, resid, scale))
    for d in range(1, NZC):
        send(St.at[blk], St.at[blk], ss.at[0], sr.at[0], zc_dev((blk + d) % NZC))

    ring_event(0, 1, 0)

    arrived(Ix.at[x, 0:7], ia_r.at[0])
    for dx in range(1, NX):
        send(Ix.at[x], Ix.at[x], ib_s.at[0], ib_r.at[0], dev((x + dx) % NX, z, c, y))

    ring_event(0, 1, 1)
    ring_event(0, 2, 0)
    y_forward(0, 0)

    arrived(Ix.at[0:3], ib_r.at[0])
    index = jnp.concatenate([Ix[u, 2 * v + c] for u in range(NX) for v in range(4)], axis=0).astype(I32)
    lane = lax.broadcasted_iota(I32, index.shape, 1)
    place = lax.broadcasted_iota(I32, index.shape, 0) // SKIP
    block = (place // 4) * NZC + (place % 4) * 2 + c

    def parity(u):
        u = u ^ (u >> 8)
        u = u ^ (u >> 4)
        u = u ^ (u >> 2)
        u = u ^ (u >> 1)
        return u & 1

    low = parity(index & lane)
    high = low ^ ((index >> 7) & 1)
    for b in range(NZC):
        flip = parity(block & (x * NZC + b))
        for part, bits in enumerate((low, high)):
            La[0:TABLE, b * ROWS + part * 128 : b * ROWS + part * 128 + 128] = (1 - 2 * (bits ^ flip)).astype(F32).astype(BF16)

    ring_event(0, 2, 1)
    ring_event(0, 3, 0)
    y_forward(0, 1)
    ring_event(0, 3, 1)
    ring_start(1)

    arrived(St.at[0:7], sr.at[0])
    weight = jnp.concatenate([St[b, 0:1, :] for b in range(NZC)], axis=1)
    resids = jnp.concatenate([St[b, 1:2, :] for b in range(NZC)], axis=1)
    scales = jnp.concatenate([St[b, 2:3, :] for b in range(NZC)], axis=1)

    def out_copy(dy, p, shape):
        plane = (y + NY - dy) % NY
        if shape == 0:
            where = (pl.ds(0, OFF[p]), pl.ds(BASE[p], 4 * PART[p]))
        else:
            where = (kept(p), pl.ds(0, BASE[p] + 4 * PART[p]))
        return copy(
            Gb.at[(dy,) + where], Gr.at[(x,) + where],
            g_s.at[p, shape], g_r.at[p, shape], dev(plane, z, c, y),
        )

    def pieces_of(p, shape):
        if shape == 0:
            return tuple(range(p)), pl.ds(BASE[p], 4 * PART[p])
        return (p,), pl.ds(0, BASE[p] + 4 * PART[p])

    def features(p):
        return pl.ds(BASE[p], 4 * PART[p])

    def left(dy, start, height):
        if dy == 0:
            return La.at[HEAD + start : HEAD + start + height]
        return Lb.at[dy - 1, start : start + height]

    def prepare(dy, p):
        rows = Z[q, gram_rows(p, c), :] if dy == 0 else Y[dy - 1, kept(p), :]
        scaled = rows.astype(F32) * weight
        high = scaled.astype(BF16)
        left(dy, 2 * OFF[p], PART[p])[...] = high
        left(dy, 2 * OFF[p] + PART[p], PART[p])[...] = (scaled - high.astype(F32)).astype(BF16)

    def product(dy, p):
        both = nt(left(dy, 0, 2 * PART[0])[...], Z[zl, features(p), :])
        Gm[dy, kept(0), features(p)] = both[: PART[0]] + both[PART[0] :]

    def product_last(dy):
        for p in range(2):
            both = nt(left(dy, 2 * OFF[1], 2 * PART[1])[...], Z[zl, features(p), :])
            Gm[dy, kept(1), features(p)] = both[: PART[1]] + both[PART[1] :]

    def product_own(p):
        all_rows = nt(La[0 : HEAD + 2 * PART[0]], Z[zl, features(p), :])
        Cs[:, features(p)] = all_rows[:TABLE].astype(BF16)
        for dx in (2, 1, 3):
            there = (x + dx) % NX
            send(
                Cs.at[plane_rows(there), features(p)], Cx.at[dx - 1, :, features(p)],
                cx_s.at[p], cx_r.at[p], dev(there, z, c, y),
            )
        Gs[:, features(p)] = jnp.broadcast_to(
            jnp.sum(all_rows[TABLE:HEAD], axis=0, keepdims=True), (8, 4 * PART[p])
        )
        Gm[0, kept(0), features(p)] = all_rows[HEAD : HEAD + PART[0]] + all_rows[HEAD + PART[0] :]

    def finish(dy, p, shape):
        parts, cols = pieces_of(p, shape)
        plane = (y + NY - dy) % NY
        for r in parts:
            block = Gm[dy, kept(r), cols] - nn(Cy[dy, kept(r), :], Cg[:, cols]) * (1.0 / TOTAL)

            @pl.when(plane == x)
            def _():
                Gown[kept(r), cols] = block

            @pl.when(plane != x)
            def _():
                Gb[dy, kept(r), cols] = block.astype(BF16)

        @pl.when(plane != x)
        def _():
            out_copy(dy, p, shape).start()

    def y_arrived(p, dy):
        if dy == 2:
            arrived(Y.at[1, kept(p), :], y2.at[p])
        else:
            arrived(Y.at[dy - 1, kept(p), 0 : DEPTH // 2], yr.at[p, dy // 2, 4])

    def half_rows(core):
        return pl.ds(pl.multiple_of(core * 4 * SKIP, 4 * SKIP), 4 * SKIP)

    def plane_rows(u):
        return pl.ds(pl.multiple_of(u * 4 * SKIP, 4 * SKIP), 4 * SKIP)

    def skipped_sum(p):
        total = Cs[plane_rows(x), features(p)].astype(F32)
        arrived(Cx.at[:, :, features(p)], cx_r.at[p])
        for dx in range(1, NX):
            total = total + Cx[dx - 1, :, features(p)].astype(F32)
        mine = Cg.at[half_rows(c), features(p)]
        mine[...] = total.astype(BF16)
        send(mine, mine, cg_s.at[p], cg_r.at[p], here_other)

    def c_copy(p, dy, far):
        there = dev(x, zh * 2 + (1 - zl if far else zl), c, (y + dy) % NY)
        return copy(
            CT.at[gram_rows(p, c), :], Cy.at[dy, kept(p), :], cy_s.at[p, far], cy_r.at[p, dy], there
        )

    c_targets = [(dy, far) for dy in (1, 3, 2, 0) for far in range(2) if dy or far]

    def skipped_spread(p):
        arrived(Cg.at[half_rows(1 - c), features(p)], cg_r.at[p])

        @pl.when(q == zl)
        def _():
            CT[features(p), :] = Cg[:, features(p)].T
            for dy, far in c_targets:
                c_copy(p, dy, far).start()
            Cy[0, kept(p), :] = CT[gram_rows(p, c), :]

    def skipped_arrived(p, dy):
        if dy:
            arrived(Cy.at[dy, kept(p), :], cy_r.at[p, dy])
        else:

            @pl.when(q != zl)
            def _():
                arrived(Cy.at[dy, kept(p), :], cy_r.at[p, dy])

    La[0:TABLE] = (La[0:TABLE].astype(F32) * scales).astype(BF16)
    La[TABLE:HEAD] = split_rows(resids)
    ring_event(0, 4, 0)
    y_forward(0, 2)
    sibling_arrived(0)
    prepare(0, 0)
    product_own(0)
    ring_event(1, 1, 0)
    ring_event(1, 1, 1)
    ring_event(1, 2, 0)
    y_forward(0, 3)
    ring_event(1, 2, 1)
    skipped_sum(0)
    ring_event(1, 3, 0)
    y_forward(1, 0)
    y_arrived(0, 1)
    prepare(1, 0)
    product(1, 0)
    ring_event(1, 3, 1)
    skipped_spread(0)
    y_arrived(0, 3)
    prepare(3, 0)
    product(3, 0)
    ring_event(1, 4, 0)
    y_forward(1, 1)
    sibling_arrived(1)
    product_own(1)
    for dx in range(1, NX):
        send(Gs, Grr.at[dx - 1], d_s.at[0], d_r.at[0], dev((x + dx) % NX, z, c, y))
    skipped_arrived(0, 0)
    finish(0, 0, 1)
    for dy in (1, 3):
        skipped_arrived(0, dy)
        finish(dy, 0, 1)
    y_forward(1, 2)
    y_forward(1, 3)
    y_arrived(0, 2)
    prepare(2, 0)
    product(2, 0)
    skipped_arrived(0, 2)
    finish(2, 0, 1)
    skipped_sum(1)
    product(1, 1)
    product(3, 1)
    product(2, 1)
    skipped_spread(1)
    for dy in (0, 1, 3, 2):
        finish(dy, 1, 0)
    prepare(0, 1)
    product_last(0)
    skipped_arrived(1, 0)
    finish(0, 1, 1)
    for dy in (1, 3, 2):
        y_arrived(1, dy)
        prepare(dy, 1)
        product_last(dy)
        skipped_arrived(1, dy)
        finish(dy, 1, 1)

    def natural(v):
        cuts = []
        for g in range(4):
            for p in range(2):
                start = BASE[p] + g * PART[p]
                cuts.append(v[:, start : start + PART[p]])
        return jnp.concatenate(cuts, axis=1)

    departed(Lr, ls.at[0])
    departed(Ix.at[x, 0:7], ia_s.at[0])
    departed(Ix.at[0:3], ib_s.at[0])
    departed(St.at[0:7], ss.at[0])
    for p in range(2):
        departed(Z.at[0, features(p), 0 : 7 * ROWS], zs.at[p])
        departed(Z.at[0, features(p), :], cs.at[p])
        departed(Y.at[0:2, kept(p), :], ys.at[p])
        departed(Y.at[0, kept(p), :], yf.at[p])
        departed(Cx.at[:, :, features(p)], cx_s.at[p])
        departed(Cg.at[half_rows(c), features(p)], cg_s.at[p])

    @pl.when(q == zl)
    def _():
        for p in range(2):
            departed(Cy.at[0:3, kept(p), :], cy_s.at[p, 0])
            departed(Cy.at[:, kept(p), :], cy_s.at[p, 1])

    total = Gs[...]
    arrived(Grr, d_r.at[0])
    for dx in range(1, NX):
        total = total + Grr[dx - 1]
    grad_ref[...] = (natural(total)[0:1, :] * (TOTAL ** -0.5)).reshape(COLS)
    departed(Grr, d_s.at[0])

    regions = []
    for p, shape in ((0, 1), (1, 0), (1, 1)):
        if shape == 0:
            where = (pl.ds(0, OFF[p]), pl.ds(BASE[p], 4 * PART[p]))
        else:
            where = (kept(p), pl.ds(0, BASE[p] + 4 * PART[p]))
        regions.append((p, shape, (pl.ds(0, 3),) + where))
    for p, shape, where in regions:
        arrived(Gr.at[where], g_r.at[p, shape])
    total = Gown[...]
    for dx in range(1, NX):
        total = total + Gr[(x + dx) % NX].astype(F32)
    gram_ref[...] = natural(total) * (SKETCH ** -0.5)
    for p, shape, where in regions:
        departed(Gb.at[where], g_s.at[p, shape])


def shards(features, weights, labels, sign_bits, sample_rows):
    vmem = pl.BlockSpec(memory_space=pltpu.VMEM)
    dma = pltpu.SemaphoreType.DMA
    scratch = [
        pltpu.VMEM((2, COLS, DEPTH), BF16),
        pltpu.VMEM((3, OUT, DEPTH), BF16),
        pltpu.VMEM((8, ROWS), F32),
        pltpu.VMEM((7, 8, ROWS), F32),
        pltpu.VMEM((NZC, 8, ROWS), F32),
        pltpu.VMEM((NX, NZC, SKIP, 128), F32),
        pltpu.VMEM((HEAD + 2 * OUT, DEPTH), BF16),
        pltpu.VMEM((3, 2 * OUT, DEPTH), BF16),
        pltpu.VMEM((NX * 4 * SKIP, COLS), BF16),
        pltpu.VMEM((3, 4 * SKIP, COLS), BF16),
        pltpu.VMEM((NZC * SKIP, COLS), BF16),
        pltpu.VMEM((COLS, NZC * SKIP), BF16),
        pltpu.VMEM((NY, OUT, NZC * SKIP), BF16),
        pltpu.VMEM((NY, OUT, COLS), F32),
        pltpu.VMEM((NY, OUT, COLS), BF16),
        pltpu.VMEM((OUT, COLS), F32),
        pltpu.VMEM((NX, OUT, COLS), BF16),
        pltpu.VMEM((8, COLS), F32),
        pltpu.VMEM((3, 8, COLS), F32),
        dma((2,)), dma((2, 2, 4, 2)),
        dma((2,)), dma((2,)),
        dma((2,)), dma((2, 2, 5)), dma((2,)), dma((2,)),
        dma((1,)), dma((1,)),
        dma((1,)), dma((1,)),
        dma((1,)), dma((1,)),
        dma((1,)), dma((1,)),
        dma((2,)), dma((2,)),
        dma((2,)), dma((2,)),
        dma((2, 4)), dma((2, 2)),
        dma((2, 2)), dma((2, 2)),
        dma((1,)), dma((1,)),
    ]
    gram, gradient = pl.pallas_call(
        kernel,
        out_shape=(
            jax.ShapeDtypeStruct((OUT, COLS), F32),
            jax.ShapeDtypeStruct((COLS,), F32),
        ),
        in_specs=[vmem] * 5,
        out_specs=(vmem, vmem),
        scratch_shapes=scratch,
        compiler_params=pltpu.CompilerParams(
            collective_id=0, has_side_effects=True, vmem_limit_bytes=56 * 2**20
        ),
        name="newton_sketch",
    )(
        features, weights, labels, sign_bits, sample_rows
    )
    return gram, gradient


def solution(mesh):
    placed = (P("row", "feat"), P("feat"), P("row"), P("row"), P("row"))
    return jax.shard_map(
        shards, mesh=mesh, in_specs=placed, out_specs=(P("row", "feat"), P("feat")), check_vma=False
    )
```

time: 88.9 us -> 83.4 us (0.938)
  the two profiles are of different devices: /device:TPU:17 before, /device:TPU:1 now
where the time goes in v3:
time: 83.4 us; the launch traced here: 83.2 us
  Pallas kernels  79.9 us (96%)
  local copies, waits for them, and re-layouts  2.67 us (3%)
    pallas_call x1, Pallas kernels, shards(): pl.pallas_call(kernel, out_shape=(jax.ShapeDtypeStruct((OUT, COLS), F32),...  79.9 us
    unnamed x4, local copies, waits for them, and re-layouts  2.67 us

profile of v3, /device:TPU:1, one launch (start us, length us, event | category | flops | bytes accessed | tf_op | source)
XLA Modules:
  0.0 83.2 jit_solution(9173597357432792486)
XLA Ops:
  0.6 79.9 %newton_sketch.1 = (f32[224,896]{1,0:T(8,128)}, f32[896]{0:T(1024)}) custom-call(bf16[256,896]{1,0:T(8,128)(2,1)} %x_ref.1, f32[896]{0:T(1024)} %w_ref.1, s32[256]{0:T(256)} %lab_ref.1, s32[256]{0:T(256)} %sgn_ref.1, s32[240]{0:T(256)} %smp_ref.1), custom_call_target="tpu_custom_call" | custom-call | tf_op jit(solution)/shard_map/newton_sketch/pallas_call | solution.py:515
  80.6 0.0 copy-start
  80.6 2.1 %copy.9 = f32[224,896]{1,0:T(8,128)} copy(f32[224,896]{1,0:T(8,128)} %get-tuple-element.4) | data formatting | bytes 1605632
  82.7 0.0 copy-done
  82.7 0.6 copy.10
Async XLA Ops:
  80.6 2.1 %copy-start = (f32[896]{0:T(1024)S(1)}, f32[896]{0:T(1024)}, u32[]{:S(2)}) copy-start(f32[896]{0:T(1024)} %get-tuple-element.5) | copy-start | bytes 10756

commit v4 on v3

--- a/solution.py
+++ b/solution.py
@@ -46,9 +46,9 @@
 
 def kernel(
     x_ref, w_ref, lab_ref, sgn_ref, smp_ref, gram_ref, grad_ref,
-    Z, Y, Ls, Lr, St, Ix, La, Lb, Cs, Cx, Cg, CT, Cy, Gm, Gb, Gown, Gr, Gs, Grr,
+    Z, Y, Ls, Lr, St, Ix, La, Lb, Cs, Cx, Cg, CT, Cy, Gm, Gb, Gown, Gf, Gr, Gs, Grr,
     zs, zr, cs, cr, ys, yr, y2, yf, ls, lr, ss, sr, ia_s, ia_r, ib_s, ib_r,
-    cx_s, cx_r, cg_s, cg_r, cy_r, cy_s, g_s, g_r, d_s, d_r,
+    cx_s, cx_r, cg_s, cg_r, cy_r, cy_s, g_s, g_r, f_s, f_r, d_s, d_r,
 ):
     row, feat = lax.axis_index("row"), lax.axis_index("feat")
     x, blk = row // NZC, row % NZC
@@ -193,6 +193,9 @@
 
     ring_start(0)
 
+    ring_event(0, 1, 0)
+    ring_event(0, 1, 1)
+
     logits = Ls[0:1, :]
     arrived(Lr, lr.at[0])
     for d in range(1, 8):
@@ -206,13 +209,10 @@
     for d in range(1, NZC):
         send(St.at[blk], St.at[blk], ss.at[0], sr.at[0], zc_dev((blk + d) % NZC))
 
-    ring_event(0, 1, 0)
-
     arrived(Ix.at[x, 0:7], ia_r.at[0])
     for dx in range(1, NX):
         send(Ix.at[x], Ix.at[x], ib_s.at[0], ib_r.at[0], dev((x + dx) % NX, z, c, y))
 
-    ring_event(0, 1, 1)
     ring_event(0, 2, 0)
     y_forward(0, 0)
 
@@ -247,21 +247,12 @@
     resids = jnp.concatenate([St[b, 1:2, :] for b in range(NZC)], axis=1)
     scales = jnp.concatenate([St[b, 2:3, :] for b in range(NZC)], axis=1)
 
-    def out_copy(dy, p, shape):
-        plane = (y + NY - dy) % NY
-        if shape == 0:
-            where = (pl.ds(0, OFF[p]), pl.ds(BASE[p], 4 * PART[p]))
-        else:
-            where = (kept(p), pl.ds(0, BASE[p] + 4 * PART[p]))
-        return copy(
-            Gb.at[(dy,) + where], Gr.at[(x,) + where],
-            g_s.at[p, shape], g_r.at[p, shape], dev(plane, z, c, y),
-        )
-
-    def pieces_of(p, shape):
-        if shape == 0:
-            return tuple(range(p)), pl.ds(BASE[p], 4 * PART[p])
-        return (p,), pl.ds(0, BASE[p] + 4 * PART[p])
+    def region(p, shape, half=None):
+        start, height = (0, OFF[p]) if shape == 0 else (OFF[p], PART[p])
+        width = (BASE[p], 4 * PART[p]) if shape == 0 else (0, BASE[p] + 4 * PART[p])
+        if half is not None:
+            start, height = start + half * (height // 2), height // 2
+        return (pl.ds(start, height), pl.ds(*width))
 
     def features(p):
         return pl.ds(BASE[p], 4 * PART[p])
@@ -282,10 +273,22 @@
         both = nt(left(dy, 0, 2 * PART[0])[...], Z[zl, features(p), :])
         Gm[dy, kept(0), features(p)] = both[: PART[0]] + both[PART[0] :]
 
-    def product_last(dy):
+    def product_rest():
+        height = 2 * PART[0]
+        rows = jnp.concatenate([left(dy, 0, height)[...] for dy in range(1, NY)], axis=0)
+        all_rows = nt(rows, Z[zl, features(1), :])
+        for dy in range(1, NY):
+            one = all_rows[(dy - 1) * height : dy * height]
+            Gm[dy, kept(0), features(1)] = one[: PART[0]] + one[PART[0] :]
+
+    def product_last():
+        height = 2 * PART[1]
+        rows = jnp.concatenate([left(dy, 2 * OFF[1], height)[...] for dy in range(NY)], axis=0)
         for p in range(2):
-            both = nt(left(dy, 2 * OFF[1], 2 * PART[1])[...], Z[zl, features(p), :])
-            Gm[dy, kept(1), features(p)] = both[: PART[1]] + both[PART[1] :]
+            all_rows = nt(rows, Z[zl, features(p), :])
+            for dy in range(NY):
+                one = all_rows[dy * height : (dy + 1) * height]
+                Gm[dy, kept(1), features(p)] = one[: PART[1]] + one[PART[1] :]
 
     def product_own(p):
         all_rows = nt(La[0 : HEAD + 2 * PART[0]], Z[zl, features(p), :])
@@ -301,23 +304,31 @@
         )
         Gm[0, kept(0), features(p)] = all_rows[HEAD : HEAD + PART[0]] + all_rows[HEAD + PART[0] :]
 
-    def finish(dy, p, shape):
-        parts, cols = pieces_of(p, shape)
-        plane = (y + NY - dy) % NY
-        for r in parts:
-            block = Gm[dy, kept(r), cols] - nn(Cy[dy, kept(r), :], Cg[:, cols]) * (1.0 / TOTAL)
-
-            @pl.when(plane == x)
-            def _():
-                Gown[kept(r), cols] = block
-
-            @pl.when(plane != x)
-            def _():
-                Gb[dy, kept(r), cols] = block.astype(BF16)
-
-        @pl.when(plane != x)
-        def _():
-            out_copy(dy, p, shape).start()
+    def corrected(dx, where):
+        dy = (y - x - dx + 2 * NY) % NY
+        return Gm[(dy,) + where] - nn(Cy[dy, where[0], :], Cg[:, where[1]]) * (1.0 / TOTAL)
+
+    def finish_far(p, shape):
+        whole = region(p, shape)
+        Gb[(1,) + whole] = corrected(2, whole).astype(BF16)
+        for half in range(2):
+            where = region(p, shape, half)
+            there = dev((x + 1 + 2 * half) % NX, z, c, y)
+            send(Gb.at[(1,) + where], Gf.at[where], f_s.at[p, shape], f_r.at[p, shape], there)
+        Gown[whole] = corrected(0, whole)
+
+    def finish_near(p, shape):
+        whole = region(p, shape)
+        arrived(Gf.at[whole], f_r.at[p, shape])
+        for half in range(2):
+            dx = 1 + 2 * half
+            added, plain = region(p, shape, half), region(p, shape, 1 - half)
+            Gb[(2 * half,) + added] = (corrected(dx, added) + Gf[added].astype(F32)).astype(BF16)
+            Gb[(2 * half,) + plain] = corrected(dx, plain).astype(BF16)
+            send(
+                Gb.at[(2 * half,) + whole], Gr.at[(half,) + whole],
+                g_s.at[p, shape], g_r.at[p, shape], dev((x + dx) % NX, z, c, y),
+            )
 
     def y_arrived(p, dy):
         if dy == 2:
@@ -396,35 +407,30 @@
     product_own(1)
     for dx in range(1, NX):
         send(Gs, Grr.at[dx - 1], d_s.at[0], d_r.at[0], dev((x + dx) % NX, z, c, y))
-    skipped_arrived(0, 0)
-    finish(0, 0, 1)
-    for dy in (1, 3):
-        skipped_arrived(0, dy)
-        finish(dy, 0, 1)
-    y_forward(1, 2)
-    y_forward(1, 3)
     y_arrived(0, 2)
     prepare(2, 0)
     product(2, 0)
-    skipped_arrived(0, 2)
-    finish(2, 0, 1)
+    for dy in range(NY):
+        skipped_arrived(0, dy)
+    finish_far(0, 1)
+    y_forward(1, 2)
+    y_forward(1, 3)
+    product_rest()
     skipped_sum(1)
-    product(1, 1)
-    product(3, 1)
-    product(2, 1)
+    prepare(0, 1)
+    y_arrived(1, 1)
+    prepare(1, 1)
     skipped_spread(1)
-    for dy in (0, 1, 3, 2):
-        finish(dy, 1, 0)
-    prepare(0, 1)
-    product_last(0)
-    skipped_arrived(1, 0)
-    finish(0, 1, 1)
-    for dy in (1, 3, 2):
+    finish_near(0, 1)
+    finish_far(1, 0)
+    for dy in (3, 2):
         y_arrived(1, dy)
         prepare(dy, 1)
-        product_last(dy)
+    product_last()
+    for dy in range(NY):
         skipped_arrived(1, dy)
-        finish(dy, 1, 1)
+    finish_far(1, 1)
+    finish_near(1, 0)
 
     def natural(v):
         cuts = []
@@ -459,21 +465,15 @@
     grad_ref[...] = (natural(total)[0:1, :] * (TOTAL ** -0.5)).reshape(COLS)
     departed(Grr, d_s.at[0])
 
-    regions = []
-    for p, shape in ((0, 1), (1, 0), (1, 1)):
-        if shape == 0:
-            where = (pl.ds(0, OFF[p]), pl.ds(BASE[p], 4 * PART[p]))
-        else:
-            where = (kept(p), pl.ds(0, BASE[p] + 4 * PART[p]))
-        regions.append((p, shape, (pl.ds(0, 3),) + where))
-    for p, shape, where in regions:
-        arrived(Gr.at[where], g_r.at[p, shape])
-    total = Gown[...]
-    for dx in range(1, NX):
-        total = total + Gr[(x + dx) % NX].astype(F32)
+    finish_near(1, 1)
+    regions = [(0, 1), (1, 0), (1, 1)]
+    for p, shape in regions:
+        arrived(Gr.at[(slice(None),) + region(p, shape)], g_r.at[p, shape])
+    total = Gown[...] + Gr[0].astype(F32) + Gr[1].astype(F32)
     gram_ref[...] = natural(total) * (SKETCH ** -0.5)
-    for p, shape, where in regions:
-        departed(Gb.at[where], g_s.at[p, shape])
+    for p, shape in regions:
+        departed(Gb.at[(1,) + region(p, shape)], f_s.at[p, shape])
+        departed(Gr.at[(slice(None),) + region(p, shape)], g_s.at[p, shape])
 
 
 def shards(features, weights, labels, sign_bits, sample_rows):
@@ -494,9 +494,10 @@
         pltpu.VMEM((COLS, NZC * SKIP), BF16),
         pltpu.VMEM((NY, OUT, NZC * SKIP), BF16),
         pltpu.VMEM((NY, OUT, COLS), F32),
-        pltpu.VMEM((NY, OUT, COLS), BF16),
+        pltpu.VMEM((3, OUT, COLS), BF16),
         pltpu.VMEM((OUT, COLS), F32),
-        pltpu.VMEM((NX, OUT, COLS), BF16),
+        pltpu.VMEM((OUT, COLS), BF16),
+        pltpu.VMEM((2, OUT, COLS), BF16),
         pltpu.VMEM((8, COLS), F32),
         pltpu.VMEM((3, 8, COLS), F32),
         dma((2,)), dma((2, 2, 4, 2)),
@@ -509,6 +510,7 @@
         dma((2,)), dma((2,)),
         dma((2,)), dma((2,)),
         dma((2, 4)), dma((2, 2)),
+        dma((2, 2)), dma((2, 2)),
         dma((2, 2)), dma((2, 2)),
         dma((1,)), dma((1,)),
     ]

time: 83.4 us -> 80.8 us (0.969)
  Pallas kernels: 79.9 us -> 77.4 us
    pallas_call x1, Pallas kernels: 79.9 us -> 77.4 us  [shards(): pl.pallas_call(kernel, out_shape=(jax.ShapeDtypeStruct((OUT, COLS), F32),...]
where the time goes in v4:
time: 80.8 us; the launch traced here: 80.7 us
  Pallas kernels  77.4 us (96%)
  local copies, waits for them, and re-layouts  2.67 us (3%)
    pallas_call x1, Pallas kernels, shards(): pl.pallas_call(kernel, out_shape=(jax.ShapeDtypeStruct((OUT, COLS), F32),...  77.4 us
    unnamed x4, local copies, waits for them, and re-layouts  2.67 us

profile of v4, /device:TPU:1, one launch (start us, length us, event | category | flops | bytes accessed | tf_op | source)
XLA Modules:
  0.0 80.7 jit_solution(4004841310406899623)
XLA Ops:
  0.6 77.4 %newton_sketch.1 = (f32[224,896]{1,0:T(8,128)}, f32[896]{0:T(1024)}) custom-call(bf16[256,896]{1,0:T(8,128)(2,1)} %x_ref.1, f32[896]{0:T(1024)} %w_ref.1, s32[256]{0:T(256)} %lab_ref.1, s32[256]{0:T(256)} %sgn_ref.1, s32[240]{0:T(256)} %smp_ref.1), custom_call_target="tpu_custom_call" | custom-call | tf_op jit(solution)/shard_map/newton_sketch/pallas_call | solution.py:517
  78.0 0.0 copy-start
  78.0 2.1 %copy.9 = f32[224,896]{1,0:T(8,128)} copy(f32[224,896]{1,0:T(8,128)} %get-tuple-element.4) | data formatting | bytes 1605632
  80.1 0.0 copy-done
  80.1 0.6 copy.10
Async XLA Ops:
  78.0 2.1 %copy-start = (f32[896]{0:T(1024)S(1)}, f32[896]{0:T(1024)}, u32[]{:S(2)}) copy-start(f32[896]{0:T(1024)} %get-tuple-element.5) | copy-start | bytes 10756

commit v5 on v4

--- a/solution.py
+++ b/solution.py
@@ -421,8 +421,8 @@
     y_arrived(1, 1)
     prepare(1, 1)
     skipped_spread(1)
+    finish_far(1, 0)
     finish_near(0, 1)
-    finish_far(1, 0)
     for dy in (3, 2):
         y_arrived(1, dy)
         prepare(dy, 1)

time: 80.8 us -> 80.5 us (level)
  no operation moved by 1% of the time
where the time goes in v5:
time: 80.5 us; the launch traced here: 80.3 us
  Pallas kernels  77 us (96%)
  local copies, waits for them, and re-layouts  2.67 us (3%)
    pallas_call x1, Pallas kernels, shards(): pl.pallas_call(kernel, out_shape=(jax.ShapeDtypeStruct((OUT, COLS), F32),...  77 us
    unnamed x4, local copies, waits for them, and re-layouts  2.67 us

profile of v5, /device:TPU:1, one launch (start us, length us, event | category | flops | bytes accessed | tf_op | source)
XLA Modules:
  0.0 80.3 jit_solution(14201484297499934516)
XLA Ops:
  0.6 77.0 %newton_sketch.1 = (f32[224,896]{1,0:T(8,128)}, f32[896]{0:T(1024)}) custom-call(bf16[256,896]{1,0:T(8,128)(2,1)} %x_ref.1, f32[896]{0:T(1024)} %w_ref.1, s32[256]{0:T(256)} %lab_ref.1, s32[256]{0:T(256)} %sgn_ref.1, s32[240]{0:T(256)} %smp_ref.1), custom_call_target="tpu_custom_call" | custom-call | tf_op jit(solution)/shard_map/newton_sketch/pallas_call | solution.py:517
  77.6 0.0 copy-start
  77.7 2.1 %copy.9 = f32[224,896]{1,0:T(8,128)} copy(f32[224,896]{1,0:T(8,128)} %get-tuple-element.4) | data formatting | bytes 1605632
  79.7 0.0 copy-done
  79.7 0.6 copy.10
Async XLA Ops:
  77.6 2.1 %copy-start = (f32[896]{0:T(1024)S(1)}, f32[896]{0:T(1024)}, u32[]{:S(2)}) copy-start(f32[896]{0:T(1024)} %get-tuple-element.5) | copy-start | bytes 10756
